TPU v7x, 32 devices: a whole 2x2x4 slice. The times are simulated.
32 devices in a mesh: mem: 16 (over z, y, x), lat: 2 (over core).
Axes of the slice: x: 2, y: 2, z: 4, core: 2. Of those that a mesh axis runs over, the one named last changes fastest.
Arguments:
- ensemble_height_winds: float32 [512, 3, 32, 256], P('mem', None, 'lat'), may hold values from -6 to 6
- obs_count: int32 [2, 16], P('lat'), may hold values from 16 to 128, as said below
- obs_cell: int32 [2, 16, 128], P('lat'), may hold values from 0 to 255
- obs_value: float32 [2, 16, 128], P('lat'), may hold values from -6 to 6
- obs_rinv: float32 [2, 16, 128], P('lat'), may hold values from 0.5 to 8
Outputs:
- analysis: float32 [2, 16, 512, 3, 256], P('lat', 'mem')
Inputs may be any that keep to these rules, and one draw needn't show every extreme that they name: `obs_count`: each region's count is 128, 64, 32 or 16, and some region has 128.
All inputs are finite; a program needn't handle non-finite values.
Results may differ from a plain program's by a relative error of at most 0.011.
Values may be sent and summed in bfloat16 or wider, within the bound.
A program may use at most 64 MiB of HBM per device.

v0:
```python
import math

import jax
import jax.numpy as jnp
from jax import lax
from jax.sharding import PartitionSpec as P

PATCH_EDGE_LEN = 16
NS_ITERS = 5


GRAVITY = 1.0
DEPTH = 1.0
CORIOLIS = 0.25
TIME_STEP = 0.5
EDGE_WEIGHT = 0.6
CORNER_WEIGHT = 0.35
NEWTON_SCALE = 16.0


def extended_2(shard, sides, width):
    for axis, dim in sides:
        size, length = (lax.axis_size(axis), shard.shape[dim])
        up = [(i, (i + 1) % size) for i in range(size - 1)]
        down = [(j, i) for i, j in up]
        last = lax.slice_in_dim(shard, length - width, length, axis=dim)
        initial = lax.slice_in_dim(shard, 0, width, axis=dim)
        before = lax.ppermute(last, axis, up)
        after = lax.ppermute(initial, axis, down)
        shard = jnp.concatenate([before, shard, after], axis=dim)
    return shard


def tendency(padded):
    height = padded[..., 0, :, :]
    east_wind = padded[..., 1, :, :]
    north_wind = padded[..., 2, :, :]

    def along_x(quantity):
        return (quantity[..., 1:-1, 2:] - quantity[..., 1:-1, :-2]) * 0.5

    def along_y(quantity):
        return (quantity[..., 2:, 1:-1] - quantity[..., :-2, 1:-1]) * 0.5

    east_mid = east_wind[..., 1:-1, 1:-1]
    north_mid = north_wind[..., 1:-1, 1:-1]
    flux_x = (DEPTH + height) * east_wind
    flux_y = (DEPTH + height) * north_wind
    rate_height = -(along_x(flux_x) + along_y(flux_y))
    rate_east = (
        -(east_mid * along_x(east_wind) + north_mid * along_y(east_wind))
        + CORIOLIS * north_mid
        - GRAVITY * along_x(height)
    )
    rate_north = (
        -(east_mid * along_x(north_wind) + north_mid * along_y(north_wind))
        - CORIOLIS * east_mid
        - GRAVITY * along_y(height)
    )
    return jnp.stack([rate_height, rate_east, rate_north], axis=-3)


def pad_columns(quantity):
    return jnp.pad(quantity, ((0, 0), (0, 0), (0, 0), (1, 1)))


def make_block(equivalents, number, measured, precision):
    ensemble = equivalents.shape[0]
    centre = jnp.mean(equivalents, axis=0)
    slot_ids = jnp.arange(equivalents.shape[1], dtype=jnp.int32)
    weight = jnp.where(slot_ids < number, jnp.sqrt(precision), 0.0)
    scaled = (weight[:, None] * (equivalents.T - centre[:, None]) / math.sqrt(ensemble - 1)).astype(
        jnp.bfloat16
    )
    misfit = weight * (measured - centre)
    summary = jnp.dot(misfit, scaled.astype(jnp.float32), precision=lax.Precision.HIGHEST)
    return jnp.concatenate([scaled, summary.astype(jnp.bfloat16)[None, :]], axis=0)


def centre_region(region):
    flat_state = region.reshape(region.shape[0], -1)
    ens_mean = jnp.mean(flat_state, axis=0)
    return (ens_mean, (flat_state - ens_mean).astype(jnp.bfloat16))


def analyse(neighbourhood, ens_mean, deviations):
    ensemble = deviations.shape[0]
    obs_slots = neighbourhood.shape[2] - 1
    locality = [
        [CORNER_WEIGHT, EDGE_WEIGHT, CORNER_WEIGHT],
        [EDGE_WEIGHT, 1.0, EDGE_WEIGHT],
        [CORNER_WEIGHT, EDGE_WEIGHT, CORNER_WEIGHT],
    ]
    gram_sum = jnp.zeros((ensemble, ensemble), jnp.float32)
    mean_drive = jnp.zeros((ensemble,), jnp.float32)
    for row_off in range(3):
        for col_off in range(3):
            factor = locality[row_off][col_off]
            scaled = neighbourhood[row_off, col_off, :obs_slots]
            gram_sum = gram_sum + factor * lax.dot_general(
                scaled, scaled, (((0,), (0,)), ((), ())), preferred_element_type=jnp.float32
            )
            mean_drive = mean_drive + factor * neighbourhood[row_off, col_off, obs_slots].astype(
                jnp.float32
            )
    identity = jnp.eye(ensemble, dtype=jnp.float32)
    root_half = ((identity + gram_sum) / NEWTON_SCALE).astype(jnp.bfloat16)
    root_inverse = identity.astype(jnp.bfloat16)
    product = root_half.astype(jnp.float32)
    for sweep in range(NS_ITERS):
        if sweep > 0:
            product = jnp.dot(root_inverse, root_half, preferred_element_type=jnp.float32)
        correction = (1.5 * identity - 0.5 * product).astype(jnp.bfloat16)
        if sweep + 1 < NS_ITERS:
            root_half = jnp.dot(root_half, correction, preferred_element_type=jnp.float32).astype(
                jnp.bfloat16
            )
        root_inverse = jnp.dot(correction, root_inverse, preferred_element_type=jnp.float32).astype(
            jnp.bfloat16
        )
    inverse_full = root_inverse.astype(jnp.float32)
    inner_step = jnp.dot(inverse_full, mean_drive, precision=lax.Precision.HIGHEST)
    mean_weights = jnp.dot(inverse_full, inner_step, precision=lax.Precision.HIGHEST) / NEWTON_SCALE
    transform = (
        mean_weights[:, None] / math.sqrt(ensemble - 1) + inverse_full / math.sqrt(NEWTON_SCALE)
    ).astype(jnp.bfloat16)
    return ens_mean + lax.dot_general(
        transform, deviations, (((0,), (0,)), ((), ())), preferred_element_type=jnp.float32
    )


def select_row(table, position):
    return lax.dynamic_index_in_dim(table, position, 0, keepdims=False)


def per_device(ensemble_height_winds, obs_count, obs_cell, obs_value, obs_rinv):
    ensemble_sequence, gridded_numbers, latitude_lines, columns = ensemble_height_winds.shape
    patch_sequence = columns // PATCH_EDGE_LEN
    region_cells = PATCH_EDGE_LEN * PATCH_EDGE_LEN
    mem_index = lax.axis_index("mem")

    def tendency_of(current):
        extended = extended_2(current, (("lat", 2),), 1)
        return tendency(pad_columns(extended))

    section_one = ensemble_height_winds + TIME_STEP * tendency_of(ensemble_height_winds)
    section_two = 0.75 * ensemble_height_winds + 0.25 * (
        section_one + TIME_STEP * tendency_of(section_one)
    )
    propagate_ahead = ensemble_height_winds / 3.0 + 2.0 / 3.0 * (
        section_two + TIME_STEP * tendency_of(section_two)
    )
    counts_row = obs_count[0]
    cells_row = obs_cell[0]
    values_row = obs_value[0]
    rinv_row = obs_rinv[0]
    arrived = lax.all_to_all(
        propagate_ahead.reshape(
            ensemble_sequence, gridded_numbers, latitude_lines, patch_sequence, PATCH_EDGE_LEN
        )
        .transpose(3, 0, 1, 2, 4)
        .reshape(
            patch_sequence, ensemble_sequence, gridded_numbers, latitude_lines * PATCH_EDGE_LEN
        ),
        "mem",
        split_axis=0,
        concat_axis=1,
        tiled=True,
    )
    ens_mean, deviations = centre_region(arrived[0])
    heights = deviations[:, :region_cells].astype(jnp.float32)
    equivalents = jnp.take(heights, select_row(cells_row, mem_index), axis=1)
    neighbourhood = extended_2(
        make_block(
            equivalents,
            select_row(counts_row, mem_index),
            select_row(values_row, mem_index),
            select_row(rinv_row, mem_index),
        )[None, None],
        (("mem", 1), ("lat", 0)),
        1,
    )
    analysed = analyse(neighbourhood, ens_mean, deviations)
    return analysed.reshape(deviations.shape[0], gridded_numbers, region_cells)[None, None]


def solution(mesh):
    in_specs = (
        P("mem", None, "lat", None),
        P("lat", None),
        P("lat", None, None),
        P("lat", None, None),
        P("lat", None, None),
    )
    out_specs = P("lat", "mem", None, None, None)
    return jax.shard_map(
        per_device, mesh=mesh, in_specs=in_specs, out_specs=out_specs, check_vma=False
    )
```

profile of v0, /device:TPU:13, one launch (start us, length us, event | category | flops | bytes accessed | tf_op | source)
XLA Modules:
  0.0 160.1 jit_solution(10372797129640393332)
XLA Ops:
  0.0 5.1 %copy.83 = f32[32,3,16,256]{0,3,2,1:T(8,128)} copy(f32[32,3,16,256]{3,2,1,0:T(8,128)} %param.5) | data formatting | bytes 3145728 | tf_op args[0]
  7.6 3.1 %collective-permute-start.1 = (f32[32,3,1,256]{0,3,2,1:T(8,128)S(1)}, f32[32,3,1,256]{0,3,2,1:T(8,128)S(1)}, u32[]{:S(2)}, u32[]{:S(2)}) collective-permute-start(f32[32,3,1,256]{0,3,2,1:T(8,128)S(1)} %get-tuple-element.31), channel_id=1, source_target_pairs={{1,0},{3,2},{5,4},{7,6},{9,8},{11,10},{13,12},{15,14},{17,16},{19,... | collective-permute-start | bytes 294920 | tf_op jit(solution)/shard_map/ppermute | solution.py:29
  12.0 4.3 %select_maximum_fusion.4 = f32[32,3,18,258]{0,3,2,1:T(8,128)S(1)} fusion(f32[32,3,1,256]{0,3,2,1:T(8,128)S(1)} %collective-permute-done.1, f32[32,3,16,256]{0,3,2,1:T(8,128)} %copy.83, f32[32,3,1,256]{0,3,2,1:T(8,128)S(1)} %collective-permute-done), kind=kLoop, calls=%fused_computation.7 | loop fusion | flops 3566592 | bytes 3552768 | tf_op jit(solution)/shard_map/concatenate | solution.py:30
  17.8 3.9 %fusion.68 = (f32[32,1,16,256]{0,3,2,1:T(8,128)S(1)}, f32[32,1,16,256]{0,3,2,1:T(8,128)S(1)}) fusion(f32[32,18,258]{0,2,1:T(8,128)S(1)} %get-tuple-element.24, f32[32,18,258]{0,2,1:T(8,128)S(1)} %get-tuple-element.23, f32[32,18,258]{0,2,1:T(8,128)S(1)} %get-tuple-element.25), kind=kLoop, calls=%fused_computation.120 | loop fusion | flops 3407872 | bytes 8388608 | tf_op jit(solution)/shard_map/stack | solution.py:60
  25.1 3.3 %collective-permute-start.3 = (f32[32,3,1,256]{0,3,2,1:T(8,128)S(1)}, f32[32,3,1,256]{0,3,2,1:T(8,128)S(1)}, u32[]{:S(2)}, u32[]{:S(2)}) collective-permute-start(f32[32,3,1,256]{0,3,2,1:T(8,128)S(1)} %get-tuple-element.29), channel_id=1, source_target_pairs={{1,0},{3,2},{5,4},{7,6},{9,8},{11,10},{13,12},{15,14},{17,16},{19,... | collective-permute-start | bytes 294920 | tf_op jit(solution)/shard_map/ppermute | solution.py:29
  29.5 2.4 %select_maximum_fusion.2 = f32[32,3,18,258]{0,3,2,1:T(8,128)S(1)} fusion(f32[32,3,1,256]{0,3,2,1:T(8,128)S(1)} %collective-permute-done.3, f32[32,3,16,256]{0,3,2,1:T(8,128)S(1)} %fusion.1, f32[32,3,1,256]{0,3,2,1:T(8,128)S(1)} %collective-permute-done.2), kind=kLoop, calls=%fused_computation.5 | loop fusion | flops 3566592 | bytes 3552768 | tf_op jit(solution)/shard_map/concatenate | solution.py:30
  31.9 1.9 %add_multiply_fusion.3 = (f32[32,18,258]{0,2,1:T(8,128)S(1)}, f32[32,18,258]{0,2,1:T(8,128)}) fusion(f32[32,3,18,258]{0,3,2,1:T(8,128)S(1)} %select_maximum_fusion.2), kind=kLoop, calls=%fused_computation.37 | loop fusion | flops 445824 | bytes 2972160 | tf_op jit(solution)/shard_map/mul | solution.py:47
  34.2 3.0 %fusion.55 = f32[32,1,16,256]{0,3,2,1:T(8,128)S(1)} fusion(f32[32,18,258]{0,2,1:T(8,128)} %get-tuple-element.13, f32[32,18,258]{0,2,1:T(8,128)S(1)} %get-tuple-element.12), kind=kLoop, calls=%fused_computation.102 | loop fusion | flops 655360 | bytes 2621440 | tf_op jit(solution)/shard_map/stack | solution.py:60
  37.2 5.3 %fusion.44 = (f32[32,1,16,256]{0,3,2,1:T(8,128)}, f32[32,1,16,256]{0,3,2,1:T(8,128)}) fusion(f32[32,18,258]{0,2,1:T(8,128)S(1)} %get-tuple-element.17, f32[32,18,258]{0,2,1:T(8,128)S(1)} %get-tuple-element.16, f32[32,18,258]{0,2,1:T(8,128)S(1)} %get-tuple-element.18), kind=kLoop, calls=%fused_computation.88 | loop fusion | flops 3407872 | bytes 8388608 | tf_op jit(solution)/shard_map/stack | solution.py:60
  42.5 4.0 %fusion.4 = f32[32,3,16,256]{0,3,2,1:T(8,128)S(1)} fusion(f32[32,1,16,256]{0,3,2,1:T(8,128)} %get-tuple-element.15, f32[32,1,16,256]{0,3,2,1:T(8,128)} %get-tuple-element.14, f32[32,1,16,256]{0,3,2,1:T(8,128)S(1)} %fusion.55, f32[32,3,16,256]{0,3,2,1:T(8,128)S(1)} %bitcast.158, f32[32,1,16,256]{0,3,2,1:T(8,128)S(1)} %copy-done.8, ...), kind=kLoop, calls=%fused_computation.15 | loop fusion | flops 4325376 | bytes 6291456 | tf_op jit(solution)/shard_map/add | solution.py:147
  47.9 3.3 %collective-permute-start.5 = (f32[32,3,1,256]{0,3,2,1:T(8,128)S(1)}, f32[32,3,1,256]{0,3,2,1:T(8,128)S(1)}, u32[]{:S(2)}, u32[]{:S(2)}) collective-permute-start(f32[32,3,1,256]{0,3,2,1:T(8,128)S(1)} %get-tuple-element.27), channel_id=1, source_target_pairs={{1,0},{3,2},{5,4},{7,6},{9,8},{11,10},{13,12},{15,14},{17,16},{19,... | collective-permute-start | bytes 294920 | tf_op jit(solution)/shard_map/ppermute | solution.py:29
  52.3 2.4 %select_maximum_fusion = f32[32,3,18,258]{0,3,2,1:T(8,128)S(1)} fusion(f32[32,3,1,256]{0,3,2,1:T(8,128)S(1)} %collective-permute-done.5, f32[32,3,16,256]{0,3,2,1:T(8,128)S(1)} %fusion.4, f32[32,3,1,256]{0,3,2,1:T(8,128)S(1)} %collective-permute-done.4), kind=kLoop, calls=%fused_computation.3 | loop fusion | flops 3566592 | bytes 3552768 | tf_op jit(solution)/shard_map/concatenate | solution.py:30
  54.8 1.8 %add_multiply_fusion.1 = (f32[32,18,258]{0,2,1:T(8,128)S(1)}, f32[32,18,258]{0,2,1:T(8,128)}) fusion(f32[32,3,18,258]{0,3,2,1:T(8,128)S(1)} %select_maximum_fusion), kind=kLoop, calls=%fused_computation.35 | loop fusion | flops 445824 | bytes 2972160 | tf_op jit(solution)/shard_map/mul | solution.py:47
  57.0 4.3 %fusion.31 = f32[32,1,16,256]{0,3,2,1:T(8,128)} fusion(f32[32,18,258]{0,2,1:T(8,128)} %get-tuple-element.6, f32[32,18,258]{0,2,1:T(8,128)S(1)} %get-tuple-element.5), kind=kLoop, calls=%fused_computation.70 | loop fusion | flops 655360 | bytes 2621440 | tf_op jit(solution)/shard_map/stack | solution.py:60
  61.3 5.2 %fusion.20 = (f32[32,1,16,256]{0,3,2,1:T(8,128)}, f32[32,1,16,256]{0,3,2,1:T(8,128)}) fusion(f32[32,18,258]{0,2,1:T(8,128)S(1)} %get-tuple-element.10, f32[32,18,258]{0,2,1:T(8,128)S(1)} %get-tuple-element.9, f32[32,18,258]{0,2,1:T(8,128)S(1)} %get-tuple-element.11), kind=kLoop, calls=%fused_computation.56 | loop fusion | flops 3407872 | bytes 8388608 | tf_op jit(solution)/shard_map/stack | solution.py:60
  66.6 5.9 %fusion.7 = f32[32,3,16,256]{0,3,2,1:T(8,128)S(1)} fusion(f32[32,1,16,256]{0,3,2,1:T(8,128)} %get-tuple-element.8, f32[32,1,16,256]{0,3,2,1:T(8,128)} %get-tuple-element.7, f32[32,1,16,256]{0,3,2,1:T(8,128)} %fusion.31, f32[32,3,16,256]{0,3,2,1:T(8,128)S(1)} %bitcast.158, f32[32,1,16,256]{0,3,2,1:T(8,128)} %get-tuple-element.15, ...), kind=kLoop, calls=%fused_computation.19 | loop fusion | flops 7077888 | bytes 7864320 | tf_op jit(solution)/shard_map/add | solution.py:150
  72.5 3.4 %copy.89 = f32[16,32,3,16,16]{1,4,3,2,0:T(8,128)} copy(f32[16,32,3,16,16]{1,4,0,3,2:T(8,128)S(1)} %bitcast.160) | data formatting | bytes 3145728 | tf_op jit(solution)/shard_map/transpose | solution.py:161
  75.8 5.5 %copy.90 = f32[16,32,3,256]{3,1,2,0:T(8,128)} copy(f32[16,32,3,256]{1,3,2,0:T(8,128)} %bitcast.159) | data formatting | bytes 3145728 | tf_op jit(solution)/shard_map/reshape | solution.py:162
  81.4 6.6 %all-to-all-start = ((f32[16,32,3,256]{3,1,2,0:T(8,128)}), f32[16,32,3,256]{3,1,2,0:T(8,128)S(1)}, u32[]{:S(2)}, u32[]{:S(2)}) async-start(f32[16,32,3,256]{3,1,2,0:T(8,128)} %copy.90), calls=%async_computation | async-start | bytes 3145728 | tf_op jit(solution)/shard_map/all_to_all | solution.py:157
  90.0 34.9 %all-to-all-done = f32[16,32,3,256]{3,1,2,0:T(8,128)S(1)} async-done(((f32[16,32,3,256]{3,1,2,0:T(8,128)}), f32[16,32,3,256]{3,1,2,0:T(8,128)S(1)}, u32[]{:S(2)}, u32[]{:S(2)}) %all-to-all-start) | async-done | bytes 1572896 | tf_op jit(solution)/shard_map/all_to_all | solution.py:157
  130.9 2.8 %collective-permute-start.6 = (bf16[1,1,129,512]{3,2,1,0:T(8,128)(2,1)S(1)}, bf16[1,1,129,512]{3,2,1,0:T(8,128)(2,1)S(1)}, u32[]{:S(2)}, u32[]{:S(2)}) collective-permute-start(bf16[1,1,129,512]{3,2,1,0:T(8,128)(2,1)S(1)} %maximum_bitcast_fusion), channel_id=1, source_target_pairs={{0,2},{2,4},{4,6},{6,8},{8,10},{10,12},{12,14},{14,16},{16,18},{18... | collective-permute-start | bytes 396296 | tf_op jit(solution)/shard_map/ppermute | solution.py:28
  133.7 3.4 %collective-permute-start.7 = (bf16[1,1,129,512]{3,2,1,0:T(8,128)(2,1)S(1)}, bf16[1,1,129,512]{3,2,1,0:T(8,128)(2,1)S(1)}, u32[]{:S(2)}, u32[]{:S(2)}) collective-permute-start(bf16[1,1,129,512]{3,2,1,0:T(8,128)(2,1)S(1)} %maximum_bitcast_fusion), channel_id=1, source_target_pairs={{2,0},{4,2},{6,4},{8,6},{10,8},{12,10},{14,12},{16,14},{18,16},{20... | collective-permute-start | bytes 396296 | tf_op jit(solution)/shard_map/ppermute | solution.py:29
  137.6 4.1 %collective-permute-done.7 = bf16[1,1,129,512]{3,2,1,0:T(8,128)(2,1)S(1)} collective-permute-done((bf16[1,1,129,512]{3,2,1,0:T(8,128)(2,1)S(1)}, bf16[1,1,129,512]{3,2,1,0:T(8,128)(2,1)S(1)}, u32[]{:S(2)}, u32[]{:S(2)}) %collective-permute-start.7) | collective-permute-done | bytes 132128 | tf_op jit(solution)/shard_map/ppermute | solution.py:29
  143.0 3.5 %collective-permute-start.9 = (bf16[1,3,129,512]{3,2,1,0:T(8,128)(2,1)S(1)}, bf16[1,3,129,512]{3,2,1,0:T(8,128)(2,1)S(1)}, u32[]{:S(2)}, u32[]{:S(2)}) collective-permute-start(bf16[1,3,129,512]{3,2,1,0:T(8,128)(2,1)S(1)} %pad_maximum_fusion), channel_id=1, source_target_pairs={{1,0},{3,2},{5,4},{7,6},{9,8},{11,10},{13,12},{15,14},{17,16},{19,... | collective-permute-start | bytes 1188872 | tf_op jit(solution)/shard_map/ppermute | solution.py:29
  (105 shorter events, 36.2 us)
Async XLA Ops:
  0.0 88.0 %copy-start = (s32[1,16]{1,0:T(1,128)S(1)}, s32[1,16]{1,0:T(1,128)}, u32[]{:S(2)}) copy-start(s32[1,16]{1,0:T(1,128)} %param.6) | copy-start | bytes 196
  6.3 4.4 %collective-permute-start = (f32[32,3,1,256]{0,3,2,1:T(8,128)S(1)}, f32[32,3,1,256]{0,3,2,1:T(8,128)S(1)}, u32[]{:S(2)}, u32[]{:S(2)}) collective-permute-start(f32[32,3,1,256]{0,3,2,1:T(8,128)S(1)} %get-tuple-element.30), channel_id=1, source_target_pairs={{0,1},{2,3},{4,5},{6,7},{8,9},{10,11},{12,13},{14,15},{16,17},{18,... | collective-permute-start | bytes 294920 | tf_op jit(solution)/shard_map/ppermute | solution.py:28
  7.6 4.4 %collective-permute-start.1 = (f32[32,3,1,256]{0,3,2,1:T(8,128)S(1)}, f32[32,3,1,256]{0,3,2,1:T(8,128)S(1)}, u32[]{:S(2)}, u32[]{:S(2)}) collective-permute-start(f32[32,3,1,256]{0,3,2,1:T(8,128)S(1)} %get-tuple-element.31), channel_id=1, source_target_pairs={{1,0},{3,2},{5,4},{7,6},{9,8},{11,10},{13,12},{15,14},{17,16},{19,... | collective-permute-start | bytes 294920 | tf_op jit(solution)/shard_map/ppermute | solution.py:29
  17.7 4.0 %copy-start.1 = (f32[32,1,16,256]{0,3,2,1:T(8,128)}, f32[32,1,16,256]{0,3,2,1:T(8,128)S(1)}, u32[]{:S(2)}) copy-start(f32[32,1,16,256]{0,3,2,1:T(8,128)S(1)} %fusion.79) | copy-start | bytes 1572868
  17.7 4.0 %slice-start = ((s8[6291456]{0:T(1024)(128)(4,1)}), s8[4194304]{0:T(1024)(128)(4,1)S(1)}, s32[]{:S(2)}) async-start(s8[6291456]{0:T(1024)(128)(4,1)} %bitcast.157), calls=%async_computation.1 | async-start | bytes 8388608
  17.7 4.0 %slice-start.1 = ((s8[6291456]{0:T(1024)(128)(4,1)}), s8[2097152]{0:T(1024)(128)(4,1)S(1)}, s32[]{:S(2)}) async-start(s8[6291456]{0:T(1024)(128)(4,1)} %bitcast.157), calls=%async_computation.2 | async-start | bytes 4194304
  23.8 4.6 %collective-permute-start.2 = (f32[32,3,1,256]{0,3,2,1:T(8,128)S(1)}, f32[32,3,1,256]{0,3,2,1:T(8,128)S(1)}, u32[]{:S(2)}, u32[]{:S(2)}) collective-permute-start(f32[32,3,1,256]{0,3,2,1:T(8,128)S(1)} %get-tuple-element.28), channel_id=1, source_target_pairs={{0,1},{2,3},{4,5},{6,7},{8,9},{10,11},{12,13},{14,15},{16,17},{18,... | collective-permute-start | bytes 294920 | tf_op jit(solution)/shard_map/ppermute | solution.py:28
  25.1 4.4 %collective-permute-start.3 = (f32[32,3,1,256]{0,3,2,1:T(8,128)S(1)}, f32[32,3,1,256]{0,3,2,1:T(8,128)S(1)}, u32[]{:S(2)}, u32[]{:S(2)}) collective-permute-start(f32[32,3,1,256]{0,3,2,1:T(8,128)S(1)} %get-tuple-element.29), channel_id=1, source_target_pairs={{1,0},{3,2},{5,4},{7,6},{9,8},{11,10},{13,12},{15,14},{17,16},{19,... | collective-permute-start | bytes 294920 | tf_op jit(solution)/shard_map/ppermute | solution.py:29
  37.2 5.3 %copy-start.10 = (f32[32,1,16,256]{0,3,2,1:T(8,128)}, f32[32,1,16,256]{0,3,2,1:T(8,128)S(1)}, u32[]{:S(2)}) copy-start(f32[32,1,16,256]{0,3,2,1:T(8,128)S(1)} %fusion.55) | copy-start | bytes 1572868
  37.2 5.3 %copy-start.2 = (f32[32,1,16,256]{0,3,2,1:T(8,128)S(1)}, f32[32,1,16,256]{0,3,2,1:T(8,128)}, u32[]{:S(2)}) copy-start(f32[32,1,16,256]{0,3,2,1:T(8,128)} %copy-done.1) | copy-start | bytes 1572868
  37.2 5.3 %copy-start.5 = (f32[32,1,16,256]{0,3,2,1:T(8,128)S(1)}, f32[32,1,16,256]{0,3,2,1:T(8,128)}, u32[]{:S(2)}) copy-start(f32[32,1,16,256]{0,3,2,1:T(8,128)} %copy-done.4) | copy-start | bytes 1572868
  37.2 5.3 %copy-start.8 = (f32[32,1,16,256]{0,3,2,1:T(8,128)S(1)}, f32[32,1,16,256]{0,3,2,1:T(8,128)}, u32[]{:S(2)}) copy-start(f32[32,1,16,256]{0,3,2,1:T(8,128)} %copy-done.7) | copy-start | bytes 1572868
  46.6 4.6 %collective-permute-start.4 = (f32[32,3,1,256]{0,3,2,1:T(8,128)S(1)}, f32[32,3,1,256]{0,3,2,1:T(8,128)S(1)}, u32[]{:S(2)}, u32[]{:S(2)}) collective-permute-start(f32[32,3,1,256]{0,3,2,1:T(8,128)S(1)} %get-tuple-element.26), channel_id=1, source_target_pairs={{0,1},{2,3},{4,5},{6,7},{8,9},{10,11},{12,13},{14,15},{16,17},{18,... | collective-permute-start | bytes 294920 | tf_op jit(solution)/shard_map/ppermute | solution.py:28
  47.9 4.4 %collective-permute-start.5 = (f32[32,3,1,256]{0,3,2,1:T(8,128)S(1)}, f32[32,3,1,256]{0,3,2,1:T(8,128)S(1)}, u32[]{:S(2)}, u32[]{:S(2)}) collective-permute-start(f32[32,3,1,256]{0,3,2,1:T(8,128)S(1)} %get-tuple-element.27), channel_id=1, source_target_pairs={{1,0},{3,2},{5,4},{7,6},{9,8},{11,10},{13,12},{15,14},{17,16},{19,... | collective-permute-start | bytes 294920 | tf_op jit(solution)/shard_map/ppermute | solution.py:29
  61.3 5.2 %copy-start.3 = (f32[32,1,16,256]{0,3,2,1:T(8,128)S(1)}, f32[32,1,16,256]{0,3,2,1:T(8,128)}, u32[]{:S(2)}) copy-start(f32[32,1,16,256]{0,3,2,1:T(8,128)} %copy-done.1) | copy-start | bytes 1572868
  61.3 5.2 %copy-start.6 = (f32[32,1,16,256]{0,3,2,1:T(8,128)S(1)}, f32[32,1,16,256]{0,3,2,1:T(8,128)}, u32[]{:S(2)}) copy-start(f32[32,1,16,256]{0,3,2,1:T(8,128)} %copy-done.4) | copy-start | bytes 1572868
  61.3 5.2 %copy-start.9 = (f32[32,1,16,256]{0,3,2,1:T(8,128)S(1)}, f32[32,1,16,256]{0,3,2,1:T(8,128)}, u32[]{:S(2)}) copy-start(f32[32,1,16,256]{0,3,2,1:T(8,128)} %copy-done.7) | copy-start | bytes 1572868
  61.3 5.2 %copy-start.11 = (f32[32,1,16,256]{0,3,2,1:T(8,128)S(1)}, f32[32,1,16,256]{0,3,2,1:T(8,128)}, u32[]{:S(2)}) copy-start(f32[32,1,16,256]{0,3,2,1:T(8,128)} %copy-done.10) | copy-start | bytes 1572868
  81.4 43.4 %all-to-all-start = ((f32[16,32,3,256]{3,1,2,0:T(8,128)}), f32[16,32,3,256]{3,1,2,0:T(8,128)S(1)}, u32[]{:S(2)}, u32[]{:S(2)}) async-start(f32[16,32,3,256]{3,1,2,0:T(8,128)} %copy.90), calls=%async_computation | async-start | bytes 3145728 | tf_op jit(solution)/shard_map/all_to_all | solution.py:157
  130.9 6.7 %collective-permute-start.6 = (bf16[1,1,129,512]{3,2,1,0:T(8,128)(2,1)S(1)}, bf16[1,1,129,512]{3,2,1,0:T(8,128)(2,1)S(1)}, u32[]{:S(2)}, u32[]{:S(2)}) collective-permute-start(bf16[1,1,129,512]{3,2,1,0:T(8,128)(2,1)S(1)} %maximum_bitcast_fusion), channel_id=1, source_target_pairs={{0,2},{2,4},{4,6},{6,8},{8,10},{10,12},{12,14},{14,16},{16,18},{18... | collective-permute-start | bytes 396296 | tf_op jit(solution)/shard_map/ppermute | solution.py:28
  133.7 8.0 %collective-permute-start.7 = (bf16[1,1,129,512]{3,2,1,0:T(8,128)(2,1)S(1)}, bf16[1,1,129,512]{3,2,1,0:T(8,128)(2,1)S(1)}, u32[]{:S(2)}, u32[]{:S(2)}) collective-permute-start(bf16[1,1,129,512]{3,2,1,0:T(8,128)(2,1)S(1)} %maximum_bitcast_fusion), channel_id=1, source_target_pairs={{2,0},{4,2},{6,4},{8,6},{10,8},{12,10},{14,12},{16,14},{18,16},{20... | collective-permute-start | bytes 396296 | tf_op jit(solution)/shard_map/ppermute | solution.py:29
  141.7 6.8 %collective-permute-start.8 = (bf16[1,3,129,512]{3,2,1,0:T(8,128)(2,1)S(1)}, bf16[1,3,129,512]{3,2,1,0:T(8,128)(2,1)S(1)}, u32[]{:S(2)}, u32[]{:S(2)}) collective-permute-start(bf16[1,3,129,512]{3,2,1,0:T(8,128)(2,1)S(1)} %pad_maximum_fusion), channel_id=1, source_target_pairs={{0,1},{2,3},{4,5},{6,7},{8,9},{10,11},{12,13},{14,15},{16,17},{18,... | collective-permute-start | bytes 1188872 | tf_op jit(solution)/shard_map/ppermute | solution.py:28
  143.0 4.6 %collective-permute-start.9 = (bf16[1,3,129,512]{3,2,1,0:T(8,128)(2,1)S(1)}, bf16[1,3,129,512]{3,2,1,0:T(8,128)(2,1)S(1)}, u32[]{:S(2)}, u32[]{:S(2)}) collective-permute-start(bf16[1,3,129,512]{3,2,1,0:T(8,128)(2,1)S(1)} %pad_maximum_fusion), channel_id=1, source_target_pairs={{1,0},{3,2},{5,4},{7,6},{9,8},{11,10},{13,12},{15,14},{17,16},{19,... | collective-permute-start | bytes 1188872 | tf_op jit(solution)/shard_map/ppermute | solution.py:29
  154.7 2.5 %copy-start.13 = (bf16[512,768]{1,0:T(8,128)(2,1)S(1)}, bf16[512,768]{1,0:T(8,128)(2,1)}, u32[]{:S(2)}) copy-start(bf16[512,768]{1,0:T(8,128)(2,1)} %copy-done.12) | copy-start | bytes 2359300
  (4 other events, 5.5 us)
where the time goes:
time: 162 us; the launch traced here: 160 us
  other arithmetic  49.6 us (31%)
  waiting for transfers between devices  43 us (27%)
  starting transfers between devices  31.1 us (19%)
  local copies, waits for them, and re-layouts  23.7 us (15%)
  matrix products  12 us (7%)
    all_to_all x1, waiting for transfers between devices, per_device(): lax.all_to_all(propagate_ahead.reshape(ensemble_sequence, gridded_numbers...  34.9 us
    another operation x6, other arithmetic, tendency(): return jnp.stack([rate_height, rate_east, rate_north], axis=-3)  22.2 us
    ppermute x5, starting transfers between devices, extended_2(): after = lax.ppermute(initial, axis, down)  16.5 us
    concatenate x4, other arithmetic, extended_2(): shard = jnp.concatenate([before, shard, after], axis=dim)  9.2 us
    ppermute x5, waiting for transfers between devices, extended_2(): after = lax.ppermute(initial, axis, down)  8 us
    ppermute x5, starting transfers between devices, extended_2(): before = lax.ppermute(last, axis, up)  7.93 us
    unnamed x36, local copies, waits for them, and re-layouts  7.41 us
    all_to_all x1, starting transfers between devices, per_device(): lax.all_to_all(propagate_ahead.reshape(ensemble_sequence, gridded_numbers...  6.61 us
  transfers between devices with their start and end apart: 11, of which 7 were waited for; matrix products, arithmetic and copies ran while one was open for 2% of the time, Pallas kernels for 0%

commit v1 on v0

v1 whole, which is shorter than its diff:
```python
import functools
import math

import jax
import jax.numpy as jnp
from jax import lax
from jax.experimental import pallas as pl
from jax.experimental.pallas import tpu as pltpu
from jax.sharding import PartitionSpec as P

PATCH_EDGE_LEN = 16
NS_ITERS = 5
GRAVITY = 1.0
DEPTH = 1.0
CORIOLIS = 0.25
TIME_STEP = 0.5
LOCALITY = (0.35, 0.6, 1.0)
NEWTON_SCALE = 16.0
HALO = 3
LANES = 128
MESH = pl.DeviceIdType.MESH
OFFSETS = [(p, q) for p in (-1, 0, 1) for q in (-1, 0, 1) if (p, q) != (0, 0)]


def split_rows(row):
    first = row.astype(jnp.bfloat16).astype(jnp.float32)
    second = (row - first).astype(jnp.bfloat16).astype(jnp.float32)
    third = row - first - second
    at = lax.broadcasted_iota(jnp.int32, (16, row.shape[1]), 0)
    rows = jnp.where(at == 0, first, jnp.where(at == 1, second, jnp.where(at == 2, third, 0.0)))
    return rows.astype(jnp.bfloat16)


def dot_nt(a, b):
    return lax.dot_general(a, b, (((1,), (1,)), ((), ())), preferred_element_type=jnp.float32)


def dot_nn(a, b):
    return jnp.dot(a, b, preferred_element_type=jnp.float32)


def step_row(src, row, group, cols):
    size = cols.shape[1]

    def at(field, i):
        return src[field, i, group, :]

    def dx(a):
        right = jnp.where(cols == size - 1, 0.0, pltpu.roll(a, size - 1, 1))
        left = jnp.where(cols == 0, 0.0, pltpu.roll(a, 1, 1))
        return right - left

    h, u, v = at(0, row), at(1, row), at(2, row)
    hm, um, vm = at(0, row - 1), at(1, row - 1), at(2, row - 1)
    hp, up, vp = at(0, row + 1), at(1, row + 1), at(2, row + 1)
    half = 0.5 * TIME_STEP
    turn = CORIOLIS * TIME_STEP
    new_h = h - half * (dx((DEPTH + h) * u) + ((DEPTH + hp) * vp - (DEPTH + hm) * vm))
    new_u = u - half * (u * dx(u) + v * (up - um) + GRAVITY * dx(h)) + turn * v
    new_v = v - half * (u * dx(v) + v * (vp - vm) + GRAVITY * (hp - hm)) - turn * u
    return new_h, new_u, new_v


def kernel(n_mem, n_lat, x_hbm, cnt, cell, val, rinv, out, xs, q, s1, s2, fin, sb, x, dev, bar, nby, nbv,
           yb, zb, mb, load_sem, halo_send, halo_recv, a2a_send, a2a_recv, nb_send, nb_recv):
    me, lat = lax.axis_index("mem"), lax.axis_index("lat")
    _, rows_ext, members, width = q.shape
    lines = rows_ext - 2 * HALO
    ensemble = x.shape[1]
    group_size = min(16, members)
    groups = [pl.ds(g * group_size, group_size) for g in range(members // group_size)]

    barrier = pltpu.get_barrier_semaphore()

    loads = [
        pltpu.make_async_copy(x_hbm.at[:, pl.ds(i * LANES, LANES)], xs.at[i], load_sem.at[i])
        for i in range(width // LANES)
    ]
    for load in loads:
        load.start()

    def greet(k, _):
        pl.semaphore_signal(barrier, inc=1, device_id=(lax.rem(me + k, n_mem), lat), device_id_type=MESH)
        return 0

    lax.fori_loop(1, n_mem, greet, 0)
    beside = [(p, q_) for p in (-1, 1) for q_ in (-1, 0, 1)]
    for p, q_ in beside:
        pl.semaphore_signal(
            barrier, inc=1,
            device_id=(lax.rem(me + q_ + n_mem, n_mem), lax.rem(lat + p + n_lat, n_lat)),
            device_id_type=MESH,
        )
    for load in loads:
        load.wait()
    stride = 3 * lines
    for i in range(width // LANES):
        for f in range(3):
            for r in range(lines):
                q[f, HALO + r, :, i * LANES:(i + 1) * LANES] = xs[i, pl.ds(f * lines + r, members, stride=stride), :]
    pl.semaphore_wait(barrier, n_mem - 1 + len(beside))

    above = (me, lax.rem(lat + n_lat - 1, n_lat))
    below = (me, lax.rem(lat + 1, n_lat))
    halos = [
        pltpu.make_async_remote_copy(
            q.at[:, pl.ds(HALO, HALO)], q.at[:, pl.ds(HALO + lines, HALO)],
            halo_send.at[0], halo_recv.at[0], device_id=above, device_id_type=MESH),
        pltpu.make_async_remote_copy(
            q.at[:, pl.ds(lines, HALO)], q.at[:, pl.ds(0, HALO)],
            halo_send.at[1], halo_recv.at[1], device_id=below, device_id_type=MESH),
    ]
    for halo in halos:
        halo.start()
    for halo in halos:
        halo.wait()

    top = jnp.where(lat > 0, 1.0, 0.0)
    bottom = jnp.where(lat < n_lat - 1, 1.0, 0.0)
    for f in range(3):
        for r in range(HALO):
            q[f, r] = q[f, r] * top
            q[f, HALO + lines + r] = q[f, HALO + lines + r] * bottom

    cols = lax.broadcasted_iota(jnp.int32, (group_size, width), 1)

    def keep(i):
        return jnp.where(i < HALO, top, jnp.where(i >= HALO + lines, bottom, 1.0))

    def first(i, _):
        for group in groups:
            for f, new in enumerate(step_row(q, i, group, cols)):
                s1[f, i, group, :] = new * keep(i)
        return 0

    def second(i, _):
        for group in groups:
            for f, new in enumerate(step_row(s1, i, group, cols)):
                s2[f, i, group, :] = (0.75 * q[f, i, group, :] + 0.25 * new) * keep(i)
        return 0

    def third(i, _):
        for group in groups:
            for f, new in enumerate(step_row(s2, i, group, cols)):
                fin[f, i - HALO, group, :] = q[f, i, group, :] * (1.0 / 3.0) + (2.0 / 3.0) * new
        return 0

    lax.fori_loop(1, rows_ext - 1, first, 0)
    lax.fori_loop(2, rows_ext - 2, second, 0)
    lax.fori_loop(3, rows_ext - 3, third, 0)

    per = LANES // PATCH_EDGE_LEN
    lane_group = lax.broadcasted_iota(jnp.int32, (group_size, LANES), 1) // PATCH_EDGE_LEN
    mine = pl.ds(pl.multiple_of(me * members, members), members)

    def part(f, k):
        target = lax.rem(me + k, n_mem)
        return pltpu.make_async_remote_copy(
            sb.at[target, f], x.at[f, mine], a2a_send.at[f, k], a2a_recv.at[f, k],
            device_id=(target, lat), device_id_type=MESH)

    for f in range(3):
        def regroup(hb, _, f=f):
            lanes = pl.ds(pl.multiple_of(hb * LANES, LANES), LANES)
            for hr in range(lines // per):
                for group in groups:
                    v = [fin[f, hr * per + i, group, lanes] for i in range(per)]
                    k = per // 2
                    while k:
                        high = (lane_group & k) > 0
                        for i in range(per):
                            if not i & k:
                                lo, hi = v[i], v[i + k]
                                v[i] = jnp.where(high, pltpu.roll(hi, PATCH_EDGE_LEN * k, 1), lo)
                                v[i + k] = jnp.where(high, hi, pltpu.roll(lo, LANES - PATCH_EDGE_LEN * k, 1))
                        k //= 2
                    for j in range(per):
                        sb[hb * per + j, f, group, hr * LANES:(hr + 1) * LANES] = v[j].astype(sb.dtype)
            return 0

        lax.fori_loop(0, width // LANES, regroup, 0)

        def send(k, _, f=f):
            part(f, k).start()
            return 0

        lax.fori_loop(1, n_mem, send, 0)
        x[f, mine, :] = sb[me, f]

    def arrive(f):
        def wait(k, _):
            part(f, k).wait()
            return 0

        lax.fori_loop(1, n_mem, wait, 0)

    def centre(f):
        total = x[f].astype(jnp.float32)
        mean = jnp.sum(total, axis=0, keepdims=True) * (1.0 / ensemble)
        bar[f] = jnp.broadcast_to(mean, bar.shape[1:])
        dev[f] = (total - mean).astype(jnp.bfloat16)

    arrive(0)
    centre(0)

    slots = cell.shape[2]
    cells = lax.broadcasted_iota(jnp.int32, (x.shape[2], slots), 0)
    one_hot = jnp.where(cells == cell[0, pl.ds(me, 1), :], 1.0, 0.0).astype(jnp.bfloat16)
    hx = dot_nn(dev[0], one_hot)
    ybar = jnp.sum(hx, axis=0, keepdims=True) * (1.0 / ensemble)
    slot = lax.broadcasted_iota(jnp.int32, (1, slots), 1)
    weight = jnp.where(slot < cnt[0, me], jnp.sqrt(rinv[0, pl.ds(me, 1), :]), 0.0)
    nby[4] = (weight * (hx - ybar) / math.sqrt(ensemble - 1)).astype(jnp.bfloat16)
    misfit = weight * (val[0, pl.ds(me, 1), :] - ybar)
    summary = jnp.sum(dot_nt(split_rows(misfit), nby[4]), axis=0, keepdims=True)
    nbv[4] = jnp.broadcast_to(summary, nbv.shape[1:]).astype(jnp.bfloat16)

    def inside(p, q_):
        return (lat + p >= 0) & (lat + p < n_lat) & (me + q_ >= 0) & (me + q_ < n_mem)

    def block(p, q_):
        slot_there = (1 - p) * 3 + (1 - q_)
        return [
            pltpu.make_async_remote_copy(
                src.at[4], src.at[slot_there], nb_send.at[i, slot_there], nb_recv.at[i, slot_there],
                device_id=(me + q_, lat + p), device_id_type=MESH)
            for i, src in enumerate((nby, nbv))
        ]

    for p, q_ in OFFSETS:
        @pl.when(inside(p, q_))
        def _(p=p, q_=q_):
            for copy in block(p, q_):
                copy.start()

    for p, q_ in OFFSETS:
        here = (1 + p) * 3 + 1 + q_

        @pl.when(inside(p, q_))
        def _(p=p, q_=q_, here=here):
            for copy in block(p, q_):
                copy.wait_send()
            for i, dst in enumerate((nby, nbv)):
                pltpu.make_async_remote_copy(
                    dst.at[4], dst.at[here], nb_send.at[i, here], nb_recv.at[i, here],
                    device_id=(me + q_, lat + p), device_id_type=MESH).wait_recv()

        @pl.when(jnp.logical_not(inside(p, q_)))
        def _(here=here):
            nby[here] = jnp.zeros(nby.shape[1:], jnp.bfloat16)
            nbv[here] = jnp.zeros(nbv.shape[1:], jnp.bfloat16)

    edges, corners = (1, 3, 5, 7), (0, 2, 6, 8)
    drive = nbv[4, 0:1, :].astype(jnp.float32)
    for i in edges:
        drive = drive + LOCALITY[1] * nbv[i, 0:1, :].astype(jnp.float32)
    for i in corners:
        drive = drive + LOCALITY[0] * nbv[i, 0:1, :].astype(jnp.float32)

    tile = ensemble // 2

    def eye(r):
        rows = lax.broadcasted_iota(jnp.int32, (tile, ensemble), 0) + r * tile
        return jnp.where(rows == lax.broadcasted_iota(jnp.int32, (tile, ensemble), 1), 1.0, 0.0)

    halves = [slice(r * tile, (r + 1) * tile) for r in range(2)]
    for r, at in enumerate(halves):
        gram = dot_nt(nby[4, at], nby[4])
        for w, which in ((LOCALITY[1], edges), (LOCALITY[0], corners)):
            left = jnp.concatenate([nby[i, at] for i in which], axis=1)
            gram = gram + w * dot_nt(left, jnp.concatenate([nby[i] for i in which], axis=1))
        root = ((eye(r) + gram) * (1.0 / NEWTON_SCALE)).astype(jnp.bfloat16)
        yb[0, at] = root
        mb[at] = (1.5 * eye(r) - 0.5 * root.astype(jnp.float32)).astype(jnp.bfloat16)

    for sweep in range(NS_ITERS):
        now, then = sweep % 2, (sweep + 1) % 2
        if sweep > 0:
            for r, at in enumerate(halves):
                product = dot_nn(yb[now, at], zb[now])
                mb[at] = (1.5 * eye(r) - 0.5 * product).astype(jnp.bfloat16)
        for at in halves:
            if sweep + 1 < NS_ITERS:
                yb[then, at] = dot_nn(mb[at], yb[now]).astype(jnp.bfloat16)
            if sweep > 0:
                zb[then, at] = dot_nn(zb[now, at], mb[...]).astype(jnp.bfloat16)
            else:
                zb[then, at] = mb[at]
    last = NS_ITERS % 2
    inner = jnp.sum(dot_nn(split_rows(drive), zb[last]), axis=0, keepdims=True)
    weights = jnp.sum(dot_nn(split_rows(inner), zb[last]), axis=0, keepdims=True) * (1.0 / NEWTON_SCALE)
    shift = weights * (1.0 / math.sqrt(ensemble - 1))
    mb[...] = (shift + zb[last].astype(jnp.float32) * (1.0 / math.sqrt(NEWTON_SCALE))).astype(jnp.bfloat16)

    for f in range(3):
        if f > 0:
            arrive(f)
            centre(f)
        out[f] = bar[f, 0:1, :] + dot_nn(mb[...], dev[f])


def per_device(n_mem, n_lat, ensemble_height_winds, obs_count, obs_cell, obs_value, obs_rinv):
    members, fields, lines, width = ensemble_height_winds.shape
    ensemble = members * n_mem
    cells = PATCH_EDGE_LEN * PATCH_EDGE_LEN
    slots = obs_cell.shape[2]
    link = jnp.bfloat16 if members % 16 == 0 else jnp.float32
    rows_ext = lines + 2 * HALO
    vmem = pl.BlockSpec(memory_space=pltpu.VMEM)
    dma = pltpu.SemaphoreType.DMA
    out = pl.pallas_call(
        functools.partial(kernel, n_mem, n_lat),
        out_shape=jax.ShapeDtypeStruct((fields, ensemble, cells), jnp.float32),
        in_specs=[
            pl.BlockSpec(memory_space=pl.ANY),
            pl.BlockSpec(memory_space=pltpu.SMEM),
            vmem, vmem, vmem,
        ],
        out_specs=vmem,
        scratch_shapes=[
            pltpu.VMEM((width // LANES, members * fields * lines, LANES), jnp.float32),
            pltpu.VMEM((fields, rows_ext, members, width), jnp.float32),
            pltpu.VMEM((fields, rows_ext, members, width), jnp.float32),
            pltpu.VMEM((fields, rows_ext, members, width), jnp.float32),
            pltpu.VMEM((fields, lines, members, width), jnp.float32),
            pltpu.VMEM((n_mem, fields, members, cells), link),
            pltpu.VMEM((fields, ensemble, cells), link),
            pltpu.VMEM((fields, ensemble, cells), jnp.bfloat16),
            pltpu.VMEM((fields, 8, cells), jnp.float32),
            pltpu.VMEM((9, ensemble, slots), jnp.bfloat16),
            pltpu.VMEM((9, 16, ensemble), jnp.bfloat16),
            pltpu.VMEM((2, ensemble, ensemble), jnp.bfloat16),
            pltpu.VMEM((2, ensemble, ensemble), jnp.bfloat16),
            pltpu.VMEM((ensemble, ensemble), jnp.bfloat16),
            dma((width // LANES,)),
            dma((2,)), dma((2,)),
            dma((fields, n_mem)), dma((fields, n_mem)),
            dma((2, 9)), dma((2, 9)),
        ],
        compiler_params=pltpu.CompilerParams(
            collective_id=0, has_side_effects=True, vmem_limit_bytes=48 * 1024 * 1024
        ),
    )(
        ensemble_height_winds.reshape(members * fields * lines, width),
        obs_count, obs_cell, obs_value, obs_rinv,
    )
    return out.transpose(1, 0, 2)[None, None]


def solution(mesh):
    in_specs = (
        P("mem", None, "lat", None),
        P("lat", None),
        P("lat", None, None),
        P("lat", None, None),
        P("lat", None, None),
    )
    out_specs = P("lat", "mem", None, None, None)
    return jax.shard_map(
        functools.partial(per_device, mesh.shape["mem"], mesh.shape["lat"]),
        mesh=mesh, in_specs=in_specs, out_specs=out_specs, check_vma=False
    )
```

time: 162 us -> 56.2 us (0.35)
  Pallas kernels: 0 us -> 50.5 us
  other arithmetic: 49.6 us -> 0 us
  waiting for transfers between devices: 43 us -> 0 us
  starting transfers between devices: 31.1 us -> 0 us
  local copies, waits for them, and re-layouts: 23.7 us -> 5.3 us
  matrix products: 12 us -> 0 us
    pallas_call x0 -> x1, Pallas kernels: none -> 50.5 us  [per_device(): pl.pallas_call(functools.partial(kernel, n_mem, n_lat), out_shape=jax.Sha...]
    all_to_all x1 -> x0, waiting for transfers between devices: 34.9 us -> none  [per_device(): lax.all_to_all(propagate_ahead.reshape(ensemble_sequence, gridded_numbers...]
    ppermute x10 -> x0, starting transfers between devices: 24.5 us -> none  [the longest x5 16.5 us: extended_2(): after = lax.ppermute(initial, axis, down)]
    another operation x7 -> x0, other arithmetic: 22.4 us -> none  [the longest x6 22.2 us: tendency(): return jnp.stack([rate_height, rate_east, rate_north], axis=-3)]
    dot_general x25 -> x0, matrix products: 12 us -> none  [the longest x9 3.13 us: analyse(): lax.dot_general(scaled, scaled, (((0,), (0,)), ((), ())), preferred_eleme...]
    add x3 -> x0, other arithmetic: 10.9 us -> none  [the longest x1 5.89 us: per_device(): ensemble_height_winds / 3.0]
    concatenate x4 -> x0, other arithmetic: 9.2 us -> none  [extended_2(): shard = jnp.concatenate([before, shard, after], axis=dim)]
    ppermute x10 -> x0, waiting for transfers between devices: 8.19 us -> none  [the longest x5 8 us: extended_2(): after = lax.ppermute(initial, axis, down)]
  transfers between devices with their start and end apart: 11 -> 0, of which waited for: 7 -> 0; matrix products, arithmetic and copies ran while one was open for 2% -> 0% of each run, Pallas kernels for 0% -> 0%
where the time goes in v1:
time: 56.2 us; the launch traced here: 55.8 us
  Pallas kernels  50.5 us (90%)
  local copies, waits for them, and re-layouts  5.3 us (9%)
    pallas_call x1, Pallas kernels, per_device(): pl.pallas_call(functools.partial(kernel, n_mem, n_lat), out_shape=jax.Sha...  50.5 us
    unnamed x11, local copies, waits for them, and re-layouts  5.3 us

profile of v1, /device:TPU:13, one launch (start us, length us, event | category | flops | bytes accessed | tf_op | source)
XLA Modules:
  0.0 55.8 jit_solution(2433499095239506788)
XLA Ops:
  0.0 0.0 copy-start
  0.0 1.4 %copy-done = f32[32,3,16,256]{3,2,1,0:T(8,128)S(1)} copy-done((f32[32,3,16,256]{3,2,1,0:T(8,128)S(1)}, f32[32,3,16,256]{3,2,1,0:T(8,128)}, u32[]{:S(2)}) %copy-start) | copy-done | bytes 1572888
  1.4 0.0 copy-start.1
  1.4 0.7 %copy-done.1 = s32[1,16,128]{2,1,0:T(8,128)S(1)} copy-done((s32[1,16,128]{2,1,0:T(8,128)S(1)}, s32[1,16,128]{2,1,0:T(8,128)}, u32[]{:S(2)}) %copy-start.1) | copy-done | bytes 8216
  2.1 0.0 copy-start.2
  2.1 0.7 %copy-done.2 = f32[1,16,128]{2,1,0:T(8,128)S(1)} copy-done((f32[1,16,128]{2,1,0:T(8,128)S(1)}, f32[1,16,128]{2,1,0:T(8,128)}, u32[]{:S(2)}) %copy-start.2) | copy-done | bytes 8216
  2.8 0.0 copy-start.3
  2.8 0.7 %copy-done.3 = f32[1,16,128]{2,1,0:T(8,128)S(1)} copy-done((f32[1,16,128]{2,1,0:T(8,128)S(1)}, f32[1,16,128]{2,1,0:T(8,128)}, u32[]{:S(2)}) %copy-start.3) | copy-done | bytes 8216
  3.5 0.0 copy-start.4
  3.5 0.7 %copy-done.4 = s32[1,16]{1,0:T(1,128)S(1)} copy-done((s32[1,16]{1,0:T(1,128)S(1)}, s32[1,16]{1,0:T(1,128)}, u32[]{:S(2)}) %copy-start.4) | copy-done | bytes 88
  4.2 50.5 %shard_map.55 = f32[3,512,256]{2,1,0:T(8,128)S(1)} custom-call(f32[1536,256]{1,0:T(8,128)S(1)} %bitcast.5, s32[1,16]{1,0:T(1,128)S(1)} %copy-done.4, s32[1,16,128]{2,1,0:T(8,128)S(1)} %copy-done.1, f32[1,16,128]{2,1,0:T(8,128)S(1)} %copy-done.2, f32[1,16,128]{2,1,0:T(8,128)S(1)} %copy-done.3), custom_call_target="tpu_custom_call" | custom-call | tf_op jit(solution)/shard_map/pallas_call | solution.py:311
  54.7 1.1 %copy.7 = f32[1,1,512,3,256]{4,2,3,1,0:T(8,128)} copy(f32[1,1,512,3,256]{4,2,3,1,0:T(8,128)S(1)} %bitcast.4) | data formatting | bytes 3145728
Async XLA Ops:
  0.0 1.4 %copy-start = (f32[32,3,16,256]{3,2,1,0:T(8,128)S(1)}, f32[32,3,16,256]{3,2,1,0:T(8,128)}, u32[]{:S(2)}) copy-start(f32[32,3,16,256]{3,2,1,0:T(8,128)} %param.5) | copy-start | bytes 4718596
  1.4 0.7 %copy-start.1 = (s32[1,16,128]{2,1,0:T(8,128)S(1)}, s32[1,16,128]{2,1,0:T(8,128)}, u32[]{:S(2)}) copy-start(s32[1,16,128]{2,1,0:T(8,128)} %cell.1) | copy-start | bytes 24580
  2.1 0.7 %copy-start.2 = (f32[1,16,128]{2,1,0:T(8,128)S(1)}, f32[1,16,128]{2,1,0:T(8,128)}, u32[]{:S(2)}) copy-start(f32[1,16,128]{2,1,0:T(8,128)} %val.1) | copy-start | bytes 24580
  2.8 0.7 %copy-start.3 = (f32[1,16,128]{2,1,0:T(8,128)S(1)}, f32[1,16,128]{2,1,0:T(8,128)}, u32[]{:S(2)}) copy-start(f32[1,16,128]{2,1,0:T(8,128)} %rinv.1) | copy-start | bytes 24580
  3.5 0.7 %copy-start.4 = (s32[1,16]{1,0:T(1,128)S(1)}, s32[1,16]{1,0:T(1,128)}, u32[]{:S(2)}) copy-start(s32[1,16]{1,0:T(1,128)} %cnt.1) | copy-start | bytes 196

commit v2 on v1

--- a/solution.py
+++ b/solution.py
@@ -61,8 +61,8 @@
     return new_h, new_u, new_v
 
 
-def kernel(n_mem, n_lat, x_hbm, cnt, cell, val, rinv, out, xs, q, s1, s2, fin, sb, x, dev, bar, nby, nbv,
-           yb, zb, mb, load_sem, halo_send, halo_recv, a2a_send, a2a_recv, nb_send, nb_recv):
+def kernel(n_mem, n_lat, x_hbm, cnt_hbm, cell_hbm, val_hbm, rinv_hbm, mb_out, dev_out, bar_out, cnt, cell, val, rinv, xs, q, s1, s2, fin, sb, x, dev, bar, nby, nbv,
+           yb, zb, mb, out_sem, obs_sem, load_sem, halo_send, halo_recv, a2a_send, a2a_recv, nb_send, nb_recv):
     me, lat = lax.axis_index("mem"), lax.axis_index("lat")
     _, rows_ext, members, width = q.shape
     lines = rows_ext - 2 * HALO
@@ -77,6 +77,12 @@
         for i in range(width // LANES)
     ]
     for load in loads:
+        load.start()
+    obs_loads = [
+        pltpu.make_async_copy(src, dst, obs_sem.at[i])
+        for i, (src, dst) in enumerate(((cnt_hbm, cnt), (cell_hbm, cell), (val_hbm, val), (rinv_hbm, rinv)))
+    ]
+    for load in obs_loads:
         load.start()
 
     def greet(k, _):
@@ -112,84 +118,77 @@
     ]
     for halo in halos:
         halo.start()
-    for halo in halos:
-        halo.wait()
-
     top = jnp.where(lat > 0, 1.0, 0.0)
     bottom = jnp.where(lat < n_lat - 1, 1.0, 0.0)
-    for f in range(3):
-        for r in range(HALO):
-            q[f, r] = q[f, r] * top
-            q[f, HALO + lines + r] = q[f, HALO + lines + r] * bottom
-
     cols = lax.broadcasted_iota(jnp.int32, (group_size, width), 1)
 
     def keep(i):
         return jnp.where(i < HALO, top, jnp.where(i >= HALO + lines, bottom, 1.0))
 
-    def first(i, _):
-        for group in groups:
-            for f, new in enumerate(step_row(q, i, group, cols)):
-                s1[f, i, group, :] = new * keep(i)
-        return 0
-
-    def second(i, _):
-        for group in groups:
-            for f, new in enumerate(step_row(s1, i, group, cols)):
-                s2[f, i, group, :] = (0.75 * q[f, i, group, :] + 0.25 * new) * keep(i)
-        return 0
-
-    def third(i, _):
-        for group in groups:
-            for f, new in enumerate(step_row(s2, i, group, cols)):
-                fin[f, i - HALO, group, :] = q[f, i, group, :] * (1.0 / 3.0) + (2.0 / 3.0) * new
-        return 0
-
-    lax.fori_loop(1, rows_ext - 1, first, 0)
-    lax.fori_loop(2, rows_ext - 2, second, 0)
-    lax.fori_loop(3, rows_ext - 3, third, 0)
+    def first(i, group):
+        for f, new in enumerate(step_row(q, i, group, cols)):
+            s1[f, i, group, :] = new * keep(i)
+
+    def second(i, group):
+        for f, new in enumerate(step_row(s1, i, group, cols)):
+            s2[f, i, group, :] = (0.75 * q[f, i, group, :] + 0.25 * new) * keep(i)
+
+    def third(i, group):
+        for f, new in enumerate(step_row(s2, i, group, cols)):
+            fin[f, i - HALO, group, :] = q[f, i, group, :] * (1.0 / 3.0) + (2.0 / 3.0) * new
+
+    def over_rows(stage, low, high, group):
+        def pair(i, _):
+            stage(low + 2 * i, group)
+            stage(low + 2 * i + 1, group)
+            return 0
+
+        lax.fori_loop(0, (high - low) // 2, pair, 0)
 
     per = LANES // PATCH_EDGE_LEN
     lane_group = lax.broadcasted_iota(jnp.int32, (group_size, LANES), 1) // PATCH_EDGE_LEN
-    mine = pl.ds(pl.multiple_of(me * members, members), members)
-
-    def part(f, k):
+
+    def part(f, g, k):
         target = lax.rem(me + k, n_mem)
+        mine = pl.ds(pl.multiple_of(me * members + g * group_size, group_size), group_size)
         return pltpu.make_async_remote_copy(
-            sb.at[target, f], x.at[f, mine], a2a_send.at[f, k], a2a_recv.at[f, k],
+            sb.at[target, f, groups[g]], x.at[f, mine], a2a_send.at[f, g, k], a2a_recv.at[f, g, k],
             device_id=(target, lat), device_id_type=MESH)
 
-    for f in range(3):
-        def regroup(hb, _, f=f):
+    def regroup(f, g):
+        group = groups[g]
+
+        def body(hb, _):
             lanes = pl.ds(pl.multiple_of(hb * LANES, LANES), LANES)
             for hr in range(lines // per):
-                for group in groups:
-                    v = [fin[f, hr * per + i, group, lanes] for i in range(per)]
-                    k = per // 2
-                    while k:
-                        high = (lane_group & k) > 0
-                        for i in range(per):
-                            if not i & k:
-                                lo, hi = v[i], v[i + k]
-                                v[i] = jnp.where(high, pltpu.roll(hi, PATCH_EDGE_LEN * k, 1), lo)
-                                v[i + k] = jnp.where(high, hi, pltpu.roll(lo, LANES - PATCH_EDGE_LEN * k, 1))
-                        k //= 2
-                    for j in range(per):
-                        sb[hb * per + j, f, group, hr * LANES:(hr + 1) * LANES] = v[j].astype(sb.dtype)
+                v = [fin[f, hr * per + i, group, lanes] for i in range(per)]
+                k = per // 2
+                while k:
+                    high = (lane_group & k) > 0
+                    for i in range(per):
+                        if not i & k:
+                            lo, hi = v[i], v[i + k]
+                            v[i] = jnp.where(high, pltpu.roll(hi, PATCH_EDGE_LEN * k, 1), lo)
+                            v[i + k] = jnp.where(high, hi, pltpu.roll(lo, LANES - PATCH_EDGE_LEN * k, 1))
+                    k //= 2
+                for j in range(per):
+                    sb[hb * per + j, f, group, hr * LANES:(hr + 1) * LANES] = v[j].astype(sb.dtype)
             return 0
 
-        lax.fori_loop(0, width // LANES, regroup, 0)
-
-        def send(k, _, f=f):
-            part(f, k).start()
+        lax.fori_loop(0, width // LANES, body, 0)
+
+    def send(f, g):
+        def one(k, _):
+            part(f, g, k).start()
             return 0
 
-        lax.fori_loop(1, n_mem, send, 0)
-        x[f, mine, :] = sb[me, f]
+        lax.fori_loop(1, n_mem, one, 0)
+        x[f, pl.ds(pl.multiple_of(me * members + g * group_size, group_size), group_size), :] = sb[me, f, groups[g]]
 
     def arrive(f):
         def wait(k, _):
-            part(f, k).wait()
+            for g in range(len(groups)):
+                part(f, g, k).wait()
             return 0
 
         lax.fori_loop(1, n_mem, wait, 0)
@@ -200,8 +199,42 @@
         bar[f] = jnp.broadcast_to(mean, bar.shape[1:])
         dev[f] = (total - mean).astype(jnp.bfloat16)
 
+    later = []
+    for g, group in enumerate(groups):
+        over_rows(first, HALO + 1, HALO + lines - 1, group)
+        if g == 0:
+            for halo in halos:
+                halo.wait()
+            for f in range(3):
+                for r in range(HALO):
+                    q[f, r] = q[f, r] * top
+                    q[f, HALO + lines + r] = q[f, HALO + lines + r] * bottom
+
+        def edge(j, _, group=group):
+            first(j + 1, group)
+            first(j + lines + HALO - 1, group)
+            return 0
+
+        lax.fori_loop(0, HALO, edge, 0)
+        over_rows(second, 2, rows_ext - 2, group)
+        over_rows(third, 3, rows_ext - 3, group)
+        regroup(0, g)
+        send(0, g)
+        for f in (1, 2):
+            regroup(f, g)
+            if f == 1 and g + 1 < len(groups):
+                send(f, g)
+            else:
+                later.append((f, g))
+    for load in obs_loads:
+        load.wait()
+
+    def leave(f):
+        return pltpu.make_async_copy(dev.at[f], dev_out.at[f], out_sem.at[f])
+
     arrive(0)
     centre(0)
+    leave(0).start()
 
     slots = cell.shape[2]
     cells = lax.broadcasted_iota(jnp.int32, (x.shape[2], slots), 0)
@@ -209,7 +242,9 @@
     hx = dot_nn(dev[0], one_hot)
     ybar = jnp.sum(hx, axis=0, keepdims=True) * (1.0 / ensemble)
     slot = lax.broadcasted_iota(jnp.int32, (1, slots), 1)
-    weight = jnp.where(slot < cnt[0, me], jnp.sqrt(rinv[0, pl.ds(me, 1), :]), 0.0)
+    count = jnp.sum(
+        jnp.where(lax.broadcasted_iota(jnp.int32, cnt.shape, 1) == me, cnt[...], 0), axis=1, keepdims=True)
+    weight = jnp.where(slot < count, jnp.sqrt(rinv[0, pl.ds(me, 1), :]), 0.0)
     nby[4] = (weight * (hx - ybar) / math.sqrt(ensemble - 1)).astype(jnp.bfloat16)
     misfit = weight * (val[0, pl.ds(me, 1), :] - ybar)
     summary = jnp.sum(dot_nt(split_rows(misfit), nby[4]), axis=0, keepdims=True)
@@ -232,6 +267,9 @@
         def _(p=p, q_=q_):
             for copy in block(p, q_):
                 copy.start()
+
+    for f, g in sorted(later):
+        send(f, g)
 
     for p, q_ in OFFSETS:
         here = (1 + p) * 3 + 1 + q_
@@ -292,11 +330,22 @@
     shift = weights * (1.0 / math.sqrt(ensemble - 1))
     mb[...] = (shift + zb[last].astype(jnp.float32) * (1.0 / math.sqrt(NEWTON_SCALE))).astype(jnp.bfloat16)
 
+    transform_out = pltpu.make_async_copy(mb, mb_out, out_sem.at[3])
+    transform_out.start()
+    for f in (1, 2):
+        arrive(f)
+        centre(f)
+        leave(f).start()
+    means_out = pltpu.make_async_copy(bar, bar_out, out_sem.at[4])
+    means_out.start()
     for f in range(3):
-        if f > 0:
-            arrive(f)
-            centre(f)
-        out[f] = bar[f, 0:1, :] + dot_nn(mb[...], dev[f])
+        leave(f).wait()
+    transform_out.wait()
+    means_out.wait()
+
+
+def apply_transform(mb, dev, bar, out):
+    out[0] = bar[0, 0:1, :] + dot_nn(mb[...], dev[0])
 
 
 def per_device(n_mem, n_lat, ensemble_height_winds, obs_count, obs_cell, obs_value, obs_rinv):
@@ -306,18 +355,19 @@
     slots = obs_cell.shape[2]
     link = jnp.bfloat16 if members % 16 == 0 else jnp.float32
     rows_ext = lines + 2 * HALO
-    vmem = pl.BlockSpec(memory_space=pltpu.VMEM)
+    groups = members // min(16, members)
     dma = pltpu.SemaphoreType.DMA
-    out = pl.pallas_call(
+    transform, deviations, means = pl.pallas_call(
         functools.partial(kernel, n_mem, n_lat),
-        out_shape=jax.ShapeDtypeStruct((fields, ensemble, cells), jnp.float32),
-        in_specs=[
-            pl.BlockSpec(memory_space=pl.ANY),
-            pl.BlockSpec(memory_space=pltpu.SMEM),
-            vmem, vmem, vmem,
-        ],
-        out_specs=vmem,
+        out_shape=(
+            jax.ShapeDtypeStruct((ensemble, ensemble), jnp.bfloat16),
+            jax.ShapeDtypeStruct((fields, ensemble, cells), jnp.bfloat16),
+            jax.ShapeDtypeStruct((fields, 8, cells), jnp.float32),
+        ),
+        in_specs=[pl.BlockSpec(memory_space=pltpu.HBM)] * 5,
+        out_specs=[pl.BlockSpec(memory_space=pltpu.HBM)] * 3,
         scratch_shapes=[
+            *(pltpu.VMEM(a.shape, a.dtype) for a in (obs_count, obs_cell, obs_value, obs_rinv)),
             pltpu.VMEM((width // LANES, members * fields * lines, LANES), jnp.float32),
             pltpu.VMEM((fields, rows_ext, members, width), jnp.float32),
             pltpu.VMEM((fields, rows_ext, members, width), jnp.float32),
@@ -332,18 +382,31 @@
             pltpu.VMEM((2, ensemble, ensemble), jnp.bfloat16),
             pltpu.VMEM((2, ensemble, ensemble), jnp.bfloat16),
             pltpu.VMEM((ensemble, ensemble), jnp.bfloat16),
+            dma((5,)),
+            dma((4,)),
             dma((width // LANES,)),
             dma((2,)), dma((2,)),
-            dma((fields, n_mem)), dma((fields, n_mem)),
+            dma((fields, groups, n_mem)), dma((fields, groups, n_mem)),
             dma((2, 9)), dma((2, 9)),
         ],
         compiler_params=pltpu.CompilerParams(
-            collective_id=0, has_side_effects=True, vmem_limit_bytes=48 * 1024 * 1024
+            collective_id=0, has_side_effects=True, vmem_limit_bytes=62 * 1024 * 1024
         ),
     )(
         ensemble_height_winds.reshape(members * fields * lines, width),
         obs_count, obs_cell, obs_value, obs_rinv,
     )
+    out = pl.pallas_call(
+        apply_transform,
+        grid=(fields,),
+        out_shape=jax.ShapeDtypeStruct((fields, ensemble, cells), jnp.float32),
+        in_specs=[
+            pl.BlockSpec((ensemble, ensemble), lambda f: (0, 0)),
+            pl.BlockSpec((1, ensemble, cells), lambda f: (f, 0, 0)),
+            pl.BlockSpec((1, 8, cells), lambda f: (f, 0, 0)),
+        ],
+        out_specs=pl.BlockSpec((1, ensemble, cells), lambda f: (f, 0, 0)),
+    )(transform, deviations, means)
     return out.transpose(1, 0, 2)[None, None]
 
 

time: 56.2 us -> 51.7 us (0.920)
  local copies, waits for them, and re-layouts: 5.3 us -> 0 us
  Pallas kernels: 50.5 us -> 51.3 us
    unnamed x11 -> x0, local copies, waits for them, and re-layouts: 5.3 us -> none
    pallas_call x1 -> x2, Pallas kernels: 50.5 us -> 51.3 us  [the longest x1 47.6 us: per_device(): pl.pallas_call(functools.partial(kernel, n_mem, n_lat), out_shape=(jax.Sh...]
where the time goes in v2:
time: 51.7 us; the launch traced here: 51.3 us
  Pallas kernels  51.3 us (99%)
    pallas_call x1, Pallas kernels, per_device(): pl.pallas_call(functools.partial(kernel, n_mem, n_lat), out_shape=(jax.Sh...  47.6 us
    pallas_call x1, Pallas kernels, per_device(): pl.pallas_call(apply_transform, grid=(fields,), out_shape=jax.ShapeDtypeS...  3.71 us

profile of v2, /device:TPU:13, one launch (start us, length us, event | category | flops | bytes accessed | tf_op | source)
XLA Modules:
  0.0 51.3 jit_solution(6381898653390262495)
XLA Ops:
  0.0 47.6 %shard_map.55 = (bf16[512,512]{1,0:T(8,128)(2,1)}, bf16[3,512,256]{2,1,0:T(8,128)(2,1)}, f32[3,8,256]{2,1,0:T(8,128)}) custom-call(f32[1536,256]{1,0:T(8,128)} %bitcast.4, s32[1,16]{1,0:T(1,128)} %cnt_hbm.1, s32[1,16,128]{2,1,0:T(8,128)} %cell_hbm.1, f32[1,16,128]{2,1,0:T(8,128)} %val_hbm.1, f32[1,16,128]{2,1,0:T(8,128)} %rinv_hbm.1), custom_call_target="tpu_custom_call" | custom-call | tf_op jit(solution)/shard_map/pallas_call | solution.py:360
  47.6 3.7 %shard_map.56 = f32[3,512,256]{2,1,0:T(8,128)} custom-call(bf16[512,512]{1,0:T(8,128)(2,1)} %get-tuple-element.8.mb, bf16[3,512,256]{2,1,0:T(8,128)(2,1)} %get-tuple-element.9.dev, f32[3,8,256]{2,1,0:T(8,128)} %get-tuple-element.10.bar), custom_call_target="tpu_custom_call" | custom-call | tf_op jit(solution)/shard_map/pallas_call | solution.py:399

commit v3 on v2

--- a/solution.py
+++ b/solution.py
@@ -19,7 +19,6 @@
 HALO = 3
 LANES = 128
 MESH = pl.DeviceIdType.MESH
-OFFSETS = [(p, q) for p in (-1, 0, 1) for q in (-1, 0, 1) if (p, q) != (0, 0)]
 
 
 def split_rows(row):
@@ -253,40 +252,71 @@
     def inside(p, q_):
         return (lat + p >= 0) & (lat + p < n_lat) & (me + q_ >= 0) & (me + q_ < n_mem)
 
-    def block(p, q_):
-        slot_there = (1 - p) * 3 + (1 - q_)
+    def block(p, q_, source, slot_there):
         return [
             pltpu.make_async_remote_copy(
-                src.at[4], src.at[slot_there], nb_send.at[i, slot_there], nb_recv.at[i, slot_there],
+                src.at[source], src.at[slot_there], nb_send.at[i, slot_there], nb_recv.at[i, slot_there],
                 device_id=(me + q_, lat + p), device_id_type=MESH)
             for i, src in enumerate((nby, nbv))
         ]
 
-    for p, q_ in OFFSETS:
-        @pl.when(inside(p, q_))
-        def _(p=p, q_=q_):
-            for copy in block(p, q_):
+    def across(q_):
+        return block(0, q_, 4, 4 - q_)
+
+    def along(p, c):
+        return block(p, 0, 4 + c, (1 - p) * 3 + 1 + c)
+
+    def clear(here):
+        nby[here] = jnp.zeros(nby.shape[1:], jnp.bfloat16)
+        nbv[here] = jnp.zeros(nbv.shape[1:], jnp.bfloat16)
+
+    for q_ in (-1, 1):
+        @pl.when(inside(0, q_))
+        def _(q_=q_):
+            for copy in across(q_):
+                copy.start()
+
+    for p in (-1, 1):
+        @pl.when(inside(p, 0))
+        def _(p=p):
+            for copy in along(p, 0):
                 copy.start()
 
     for f, g in sorted(later):
         send(f, g)
 
-    for p, q_ in OFFSETS:
-        here = (1 + p) * 3 + 1 + q_
-
-        @pl.when(inside(p, q_))
-        def _(p=p, q_=q_, here=here):
-            for copy in block(p, q_):
+    for q_ in (-1, 1):
+        @pl.when(inside(0, q_))
+        def _(q_=q_):
+            for copy in across(q_):
                 copy.wait_send()
-            for i, dst in enumerate((nby, nbv)):
-                pltpu.make_async_remote_copy(
-                    dst.at[4], dst.at[here], nb_send.at[i, here], nb_recv.at[i, here],
-                    device_id=(me + q_, lat + p), device_id_type=MESH).wait_recv()
-
-        @pl.when(jnp.logical_not(inside(p, q_)))
-        def _(here=here):
-            nby[here] = jnp.zeros(nby.shape[1:], jnp.bfloat16)
-            nbv[here] = jnp.zeros(nbv.shape[1:], jnp.bfloat16)
+            for copy in block(0, q_, 4, 4 + q_):
+                copy.wait_recv()
+
+        @pl.when(jnp.logical_not(inside(0, q_)))
+        def _(q_=q_):
+            clear(4 + q_)
+
+    for p in (-1, 1):
+        @pl.when(inside(p, 0))
+        def _(p=p):
+            for c in (-1, 1):
+                for copy in along(p, c):
+                    copy.start()
+
+    for p in (-1, 1):
+        @pl.when(inside(p, 0))
+        def _(p=p):
+            for c in (-1, 0, 1):
+                for copy in along(p, c):
+                    copy.wait_send()
+                for copy in block(p, 0, 4 + c, (1 + p) * 3 + 1 + c):
+                    copy.wait_recv()
+
+        @pl.when(jnp.logical_not(inside(p, 0)))
+        def _(p=p):
+            for c in (-1, 0, 1):
+                clear((1 + p) * 3 + 1 + c)
 
     edges, corners = (1, 3, 5, 7), (0, 2, 6, 8)
     drive = nbv[4, 0:1, :].astype(jnp.float32)

time: 51.7 us -> 47.1 us (0.911)
  Pallas kernels: 51.3 us -> 46.5 us
    pallas_call x1, Pallas kernels: 47.6 us -> 42.8 us  [per_device(): pl.pallas_call(functools.partial(kernel, n_mem, n_lat), out_shape=(jax.Sh...]
where the time goes in v3:
time: 47.1 us; the launch traced here: 46.6 us
  Pallas kernels  46.5 us (99%)
    pallas_call x1, Pallas kernels, per_device(): pl.pallas_call(functools.partial(kernel, n_mem, n_lat), out_shape=(jax.Sh...  42.8 us
    pallas_call x1, Pallas kernels, per_device(): pl.pallas_call(apply_transform, grid=(fields,), out_shape=jax.ShapeDtypeS...  3.72 us

profile of v3, /device:TPU:13, one launch (start us, length us, event | category | flops | bytes accessed | tf_op | source)
XLA Modules:
  0.0 46.6 jit_solution(16838916116583151291)
XLA Ops:
  0.0 42.8 %shard_map.55 = (bf16[512,512]{1,0:T(8,128)(2,1)}, bf16[3,512,256]{2,1,0:T(8,128)(2,1)}, f32[3,8,256]{2,1,0:T(8,128)}) custom-call(f32[1536,256]{1,0:T(8,128)} %bitcast.4, s32[1,16]{1,0:T(1,128)} %cnt_hbm.1, s32[1,16,128]{2,1,0:T(8,128)} %cell_hbm.1, f32[1,16,128]{2,1,0:T(8,128)} %val_hbm.1, f32[1,16,128]{2,1,0:T(8,128)} %rinv_hbm.1), custom_call_target="tpu_custom_call" | custom-call | tf_op jit(solution)/shard_map/pallas_call | solution.py:390
  42.8 3.7 %shard_map.56 = f32[3,512,256]{2,1,0:T(8,128)} custom-call(bf16[512,512]{1,0:T(8,128)(2,1)} %get-tuple-element.8.mb, bf16[3,512,256]{2,1,0:T(8,128)(2,1)} %get-tuple-element.9.dev, f32[3,8,256]{2,1,0:T(8,128)} %get-tuple-element.10.bar), custom_call_target="tpu_custom_call" | custom-call | tf_op jit(solution)/shard_map/pallas_call | solution.py:429

commit v4 on v3

--- a/solution.py
+++ b/solution.py
@@ -103,20 +103,7 @@
         for f in range(3):
             for r in range(lines):
                 q[f, HALO + r, :, i * LANES:(i + 1) * LANES] = xs[i, pl.ds(f * lines + r, members, stride=stride), :]
-    pl.semaphore_wait(barrier, n_mem - 1 + len(beside))
-
-    above = (me, lax.rem(lat + n_lat - 1, n_lat))
-    below = (me, lax.rem(lat + 1, n_lat))
-    halos = [
-        pltpu.make_async_remote_copy(
-            q.at[:, pl.ds(HALO, HALO)], q.at[:, pl.ds(HALO + lines, HALO)],
-            halo_send.at[0], halo_recv.at[0], device_id=above, device_id_type=MESH),
-        pltpu.make_async_remote_copy(
-            q.at[:, pl.ds(lines, HALO)], q.at[:, pl.ds(0, HALO)],
-            halo_send.at[1], halo_recv.at[1], device_id=below, device_id_type=MESH),
-    ]
-    for halo in halos:
-        halo.start()
+
     top = jnp.where(lat > 0, 1.0, 0.0)
     bottom = jnp.where(lat < n_lat - 1, 1.0, 0.0)
     cols = lax.broadcasted_iota(jnp.int32, (group_size, width), 1)
@@ -198,9 +185,26 @@
         bar[f] = jnp.broadcast_to(mean, bar.shape[1:])
         dev[f] = (total - mean).astype(jnp.bfloat16)
 
+    for group in groups:
+        over_rows(first, HALO + 1, HALO + lines - 1, group)
+    pl.semaphore_wait(barrier, n_mem - 1 + len(beside))
+
+    above = (me, lax.rem(lat + n_lat - 1, n_lat))
+    below = (me, lax.rem(lat + 1, n_lat))
+    halos = [
+        pltpu.make_async_remote_copy(
+            q.at[:, pl.ds(HALO, HALO)], q.at[:, pl.ds(HALO + lines, HALO)],
+            halo_send.at[0], halo_recv.at[0], device_id=above, device_id_type=MESH),
+        pltpu.make_async_remote_copy(
+            q.at[:, pl.ds(lines, HALO)], q.at[:, pl.ds(0, HALO)],
+            halo_send.at[1], halo_recv.at[1], device_id=below, device_id_type=MESH),
+    ]
+    for halo in halos:
+        halo.start()
     later = []
     for g, group in enumerate(groups):
-        over_rows(first, HALO + 1, HALO + lines - 1, group)
+        over_rows(second, HALO + 2, HALO + lines - 2, group)
+        over_rows(third, HALO + 3, HALO + lines - 3, group)
         if g == 0:
             for halo in halos:
                 halo.wait()
@@ -208,15 +212,13 @@
                 for r in range(HALO):
                     q[f, r] = q[f, r] * top
                     q[f, HALO + lines + r] = q[f, HALO + lines + r] * bottom
-
-        def edge(j, _, group=group):
-            first(j + 1, group)
-            first(j + lines + HALO - 1, group)
-            return 0
-
-        lax.fori_loop(0, HALO, edge, 0)
-        over_rows(second, 2, rows_ext - 2, group)
-        over_rows(third, 3, rows_ext - 3, group)
+        for at, stage in enumerate((first, second, third)):
+            def edge(j, _, group=group, at=at, stage=stage):
+                stage(j + 1 + at, group)
+                stage(j + lines + HALO - 1 - at, group)
+                return 0
+
+            lax.fori_loop(0, HALO, edge, 0)
         regroup(0, g)
         send(0, g)
         for f in (1, 2):

time: 47.1 us -> 45.6 us (0.968)
  Pallas kernels: 46.5 us -> 45.4 us
    pallas_call x1, Pallas kernels: 42.8 us -> 41.7 us  [per_device(): pl.pallas_call(functools.partial(kernel, n_mem, n_lat), out_shape=(jax.Sh...]
where the time goes in v4:
time: 45.6 us; the launch traced here: 45.4 us
  Pallas kernels  45.4 us (100%)
    pallas_call x1, Pallas kernels, per_device(): pl.pallas_call(functools.partial(kernel, n_mem, n_lat), out_shape=(jax.Sh...  41.7 us
    pallas_call x1, Pallas kernels, per_device(): pl.pallas_call(apply_transform, grid=(fields,), out_shape=jax.ShapeDtypeS...  3.72 us

profile of v4, /device:TPU:13, one launch (start us, length us, event | category | flops | bytes accessed | tf_op | source)
XLA Modules:
  0.0 45.4 jit_solution(8649799535697719434)
XLA Ops:
  0.0 41.7 %shard_map.55 = (bf16[512,512]{1,0:T(8,128)(2,1)}, bf16[3,512,256]{2,1,0:T(8,128)(2,1)}, f32[3,8,256]{2,1,0:T(8,128)}) custom-call(f32[1536,256]{1,0:T(8,128)} %bitcast.4, s32[1,16]{1,0:T(1,128)} %cnt_hbm.1, s32[1,16,128]{2,1,0:T(8,128)} %cell_hbm.1, f32[1,16,128]{2,1,0:T(8,128)} %val_hbm.1, f32[1,16,128]{2,1,0:T(8,128)} %rinv_hbm.1), custom_call_target="tpu_custom_call" | custom-call | tf_op jit(solution)/shard_map/pallas_call | solution.py:392
  41.7 3.7 %shard_map.56 = f32[3,512,256]{2,1,0:T(8,128)} custom-call(bf16[512,512]{1,0:T(8,128)(2,1)} %get-tuple-element.8.mb, bf16[3,512,256]{2,1,0:T(8,128)(2,1)} %get-tuple-element.9.dev, f32[3,8,256]{2,1,0:T(8,128)} %get-tuple-element.10.bar), custom_call_target="tpu_custom_call" | custom-call | tf_op jit(solution)/shard_map/pallas_call | solution.py:431

commit v5 on v4

--- a/solution.py
+++ b/solution.py
@@ -60,8 +60,8 @@
     return new_h, new_u, new_v
 
 
-def kernel(n_mem, n_lat, x_hbm, cnt_hbm, cell_hbm, val_hbm, rinv_hbm, mb_out, dev_out, bar_out, cnt, cell, val, rinv, xs, q, s1, s2, fin, sb, x, dev, bar, nby, nbv,
-           yb, zb, mb, out_sem, obs_sem, load_sem, halo_send, halo_recv, a2a_send, a2a_recv, nb_send, nb_recv):
+def kernel(n_mem, n_lat, x_hbm, cnt_hbm, cell_hbm, val_hbm, rinv_hbm, out_hbm, cnt, cell, val, rinv, xs, q, s1, s2, fin, sb, x, dev, bar, nby, nbv,
+           yb, zb, mb, out, out_sem, obs_sem, load_sem, halo_send, halo_recv, a2a_send, a2a_recv, nb_send, nb_recv):
     me, lat = lax.axis_index("mem"), lax.axis_index("lat")
     _, rows_ext, members, width = q.shape
     lines = rows_ext - 2 * HALO
@@ -231,11 +231,10 @@
         load.wait()
 
     def leave(f):
-        return pltpu.make_async_copy(dev.at[f], dev_out.at[f], out_sem.at[f])
+        return pltpu.make_async_copy(out.at[f], out_hbm.at[f], out_sem.at[f])
 
     arrive(0)
     centre(0)
-    leave(0).start()
 
     slots = cell.shape[2]
     cells = lax.broadcasted_iota(jnp.int32, (x.shape[2], slots), 0)
@@ -362,22 +361,14 @@
     shift = weights * (1.0 / math.sqrt(ensemble - 1))
     mb[...] = (shift + zb[last].astype(jnp.float32) * (1.0 / math.sqrt(NEWTON_SCALE))).astype(jnp.bfloat16)
 
-    transform_out = pltpu.make_async_copy(mb, mb_out, out_sem.at[3])
-    transform_out.start()
-    for f in (1, 2):
-        arrive(f)
-        centre(f)
+    for f in range(3):
+        if f > 0:
+            arrive(f)
+            centre(f)
+        out[f] = bar[f, 0:1, :] + dot_nn(mb[...], dev[f])
         leave(f).start()
-    means_out = pltpu.make_async_copy(bar, bar_out, out_sem.at[4])
-    means_out.start()
     for f in range(3):
         leave(f).wait()
-    transform_out.wait()
-    means_out.wait()
-
-
-def apply_transform(mb, dev, bar, out):
-    out[0] = bar[0, 0:1, :] + dot_nn(mb[...], dev[0])
 
 
 def per_device(n_mem, n_lat, ensemble_height_winds, obs_count, obs_cell, obs_value, obs_rinv):
@@ -389,15 +380,11 @@
     rows_ext = lines + 2 * HALO
     groups = members // min(16, members)
     dma = pltpu.SemaphoreType.DMA
-    transform, deviations, means = pl.pallas_call(
+    out = pl.pallas_call(
         functools.partial(kernel, n_mem, n_lat),
-        out_shape=(
-            jax.ShapeDtypeStruct((ensemble, ensemble), jnp.bfloat16),
-            jax.ShapeDtypeStruct((fields, ensemble, cells), jnp.bfloat16),
-            jax.ShapeDtypeStruct((fields, 8, cells), jnp.float32),
-        ),
+        out_shape=jax.ShapeDtypeStruct((fields, ensemble, cells), jnp.float32),
         in_specs=[pl.BlockSpec(memory_space=pltpu.HBM)] * 5,
-        out_specs=[pl.BlockSpec(memory_space=pltpu.HBM)] * 3,
+        out_specs=pl.BlockSpec(memory_space=pltpu.HBM),
         scratch_shapes=[
             *(pltpu.VMEM(a.shape, a.dtype) for a in (obs_count, obs_cell, obs_value, obs_rinv)),
             pltpu.VMEM((width // LANES, members * fields * lines, LANES), jnp.float32),
@@ -414,7 +401,8 @@
             pltpu.VMEM((2, ensemble, ensemble), jnp.bfloat16),
             pltpu.VMEM((2, ensemble, ensemble), jnp.bfloat16),
             pltpu.VMEM((ensemble, ensemble), jnp.bfloat16),
-            dma((5,)),
+            pltpu.VMEM((fields, ensemble, cells), jnp.float32),
+            dma((3,)),
             dma((4,)),
             dma((width // LANES,)),
             dma((2,)), dma((2,)),
@@ -428,17 +416,6 @@
         ensemble_height_winds.reshape(members * fields * lines, width),
         obs_count, obs_cell, obs_value, obs_rinv,
     )
-    out = pl.pallas_call(
-        apply_transform,
-        grid=(fields,),
-        out_shape=jax.ShapeDtypeStruct((fields, ensemble, cells), jnp.float32),
-        in_specs=[
-            pl.BlockSpec((ensemble, ensemble), lambda f: (0, 0)),
-            pl.BlockSpec((1, ensemble, cells), lambda f: (f, 0, 0)),
-            pl.BlockSpec((1, 8, cells), lambda f: (f, 0, 0)),
-        ],
-        out_specs=pl.BlockSpec((1, ensemble, cells), lambda f: (f, 0, 0)),
-    )(transform, deviations, means)
     return out.transpose(1, 0, 2)[None, None]
 
 

time: 45.6 us -> 45.6 us (level)
  local copies, waits for them, and re-layouts: 0 us -> 2.65 us
  Pallas kernels: 45.4 us -> 42.8 us
    unnamed x0 -> x1, local copies, waits for them, and re-layouts: none -> 2.65 us
    pallas_call x2 -> x1, Pallas kernels: 45.4 us -> 42.8 us  [per_device(): pl.pallas_call(functools.partial(kernel, n_mem, n_lat), out_shape=jax.Sha...]
where the time goes in v5:
time: 45.6 us; the launch traced here: 45.5 us
  Pallas kernels  42.8 us (94%)
  local copies, waits for them, and re-layouts  2.65 us (6%)
    pallas_call x1, Pallas kernels, per_device(): pl.pallas_call(functools.partial(kernel, n_mem, n_lat), out_shape=jax.Sha...  42.8 us
    unnamed x1, local copies, waits for them, and re-layouts  2.65 us

profile of v5, /device:TPU:13, one launch (start us, length us, event | category | flops | bytes accessed | tf_op | source)
XLA Modules:
  0.0 45.5 jit_solution(1131987990523117123)
XLA Ops:
  0.0 42.8 %shard_map.55 = f32[3,512,256]{2,1,0:T(8,128)} custom-call(f32[1536,256]{1,0:T(8,128)} %bitcast.5, s32[1,16]{1,0:T(1,128)} %cnt_hbm.1, s32[1,16,128]{2,1,0:T(8,128)} %cell_hbm.1, f32[1,16,128]{2,1,0:T(8,128)} %val_hbm.1, f32[1,16,128]{2,1,0:T(8,128)} %rinv_hbm.1), custom_call_target="tpu_custom_call" | custom-call | tf_op jit(solution)/shard_map/pallas_call | solution.py:383
  42.8 2.7 %copy.7 = f32[1,1,512,3,256]{4,2,3,1,0:T(8,128)} copy(f32[1,1,512,3,256]{4,2,3,1,0:T(8,128)} %bitcast.4) | data formatting | bytes 3145728
